TPU v7x, 32 devices: a whole 2x2x4 slice. The times are simulated.
32 devices in a mesh: seq: 4 (over x, core), fsdp: 8 (over z, y).
Axes of the slice: x: 2, y: 2, z: 4, core: 2. Of those that a mesh axis runs over, the one named last changes fastest.
Arguments:
- inputs: bfloat16 [16, 1568, 1024], P('fsdp', 'seq'), may hold values from -7 to 7
- cotangent: bfloat16 [16, 1568, 1024], P('fsdp', 'seq'), may hold values from -6 to 6
- valid: int32 [16, 1568], P('fsdp'), may hold values from 0 to 1, as said below
- ln1_gain: bfloat16 [1024], P('fsdp'), may hold values from 0.25 to 1.75
- ln1_bias: bfloat16 [1024], P('fsdp'), may hold values from -1.75 to 1.75
- qkv_weight: bfloat16 [1024, 3072], P('fsdp'), may hold values from -0.1875 to 0.1875
- q_bias: bfloat16 [1024], P('fsdp'), may hold values from -3 to 3
- v_bias: bfloat16 [1024], P('fsdp'), may hold values from -0.3125 to 0.3125
- out_weight: bfloat16 [1024, 1024], P('fsdp'), may hold values from -2 to 2
- out_bias: bfloat16 [1024], P('fsdp'), may hold values from -1.75 to 1.75
- ln2_gain: bfloat16 [1024], P('fsdp'), may hold values from 0.25 to 1.75
- ln2_bias: bfloat16 [1024], P('fsdp'), may hold values from -1.75 to 1.75
- fc1_weight: bfloat16 [1024, 4096], P('fsdp'), may hold values from -0.1875 to 0.1875
- fc1_bias: bfloat16 [4096], P('fsdp'), may hold values from -1.75 to 1.75
- fc2_weight: bfloat16 [4096, 1024], P('fsdp'), may hold values from -0.09375 to 0.09375
- fc2_bias: bfloat16 [1024], P('fsdp'), may hold values from -1.75 to 1.75
Outputs:
- output: bfloat16 [16, 1568, 1024], P('fsdp', 'seq')
- input_grad: bfloat16 [16, 1568, 1024], P('fsdp', 'seq')
- ln1_gain_grad: float32 [1024], P('fsdp')
- ln1_bias_grad: float32 [1024], P('fsdp')
- qkv_weight_grad: float32 [1024, 3072], P('fsdp')
- q_bias_grad: float32 [1024], P('fsdp')
- v_bias_grad: float32 [1024], P('fsdp')
- out_weight_grad: float32 [1024, 1024], P('fsdp')
- out_bias_grad: float32 [1024], P('fsdp')
- ln2_gain_grad: float32 [1024], P('fsdp')
- ln2_bias_grad: float32 [1024], P('fsdp')
- fc1_weight_grad: float32 [1024, 4096], P('fsdp')
- fc1_bias_grad: float32 [4096], P('fsdp')
- fc2_weight_grad: float32 [4096, 1024], P('fsdp')
- fc2_bias_grad: float32 [1024], P('fsdp')
- branch_rms: float32 [3], replicated
Inputs may be any that keep to these rules, and one draw needn't show every extreme that they name: In every clip the valid tokens are a leading run of 392 tokens or more; some clip is valid in all its tokens.
All inputs are finite; a program needn't handle non-finite values.
Results may differ from a plain program's by a relative error of at most 0.015.
Values may be sent and summed in bfloat16 or wider, within the bound.
No kernel may reach another device: no remote copies, remote signals or barrier semaphores. Data moves between devices by JAX's collectives and lax.ppermute only.
A program may use at most 192 MiB of HBM per device.

v0:
```python
from functools import partial
import jax
import jax.numpy as jnp
from jax import lax
from jax.sharding import PartitionSpec as P

HEADS = 16
HEAD = 64
EPS = 1e-06
masked_score = -1e30


def layer_norm(values, gain, bias):
    center = values - jnp.mean(values, axis=-1, keepdims=True)
    spread = jnp.mean(center * center, axis=-1, keepdims=True)
    return center * lax.rsqrt(spread + EPS) * gain + bias


def gelu_exact(values):
    return jax.nn.gelu(values, approximate=False)


def contract_rows(left, right):
    return lax.dot_general(
        left, right, (((0,), (0,)), ((), ())), preferred_element_type=jnp.float32
    )


def times_transpose(left, right):
    return lax.dot_general(
        left, right, (((1,), (1,)), ((), ())), preferred_element_type=jnp.float32
    )


def column_sum(values):
    return jnp.sum(values, axis=0, dtype=jnp.float32)


def head_major(values, heads_here):
    clip_count, length, total_width = values.shape
    return jnp.moveaxis(values.reshape(clip_count, length, heads_here, HEAD), 2, 0)


def token_major(values):
    heads_here, clip_count, length, head_width = values.shape
    return jnp.moveaxis(values, 0, 2).reshape(clip_count, length, heads_here * head_width)


def attend_forward(pieces, keep):
    queries, key_rows, value_rows = pieces
    scores = jnp.einsum("cqd,ckd->cqk", queries, key_rows, preferred_element_type=jnp.float32)
    scores = jnp.where(keep[:, None, :], scores, masked_score)
    highest = jnp.max(scores, axis=-1, keepdims=True)
    weights = jnp.exp(scores - highest)
    totals = jnp.sum(weights, axis=-1, keepdims=True)
    probs_low = (weights / totals).astype(jnp.bfloat16)
    context = jnp.einsum(
        "cqk,ckd->cqd", probs_low, value_rows, preferred_element_type=jnp.float32
    ).astype(jnp.bfloat16)
    return (context, (highest + jnp.log(totals))[..., 0])


def attend_backward(pieces, keep):
    queries, key_rows, value_rows, log_total, grad_context = pieces
    scores = jnp.einsum("cqd,ckd->cqk", queries, key_rows, preferred_element_type=jnp.float32)
    scores = jnp.where(keep[:, None, :], scores, masked_score)
    probs = jnp.exp(scores - log_total[..., None])
    grad_probs = jnp.einsum(
        "cqd,ckd->cqk", grad_context, value_rows, preferred_element_type=jnp.float32
    )
    inner = jnp.sum(grad_probs * probs, axis=-1, keepdims=True)
    grad_scores = (probs * (grad_probs - inner)).astype(jnp.bfloat16)
    grad_queries = jnp.einsum(
        "cqk,ckd->cqd", grad_scores, key_rows, preferred_element_type=jnp.float32
    ).astype(jnp.bfloat16)
    grad_keys = jnp.einsum(
        "cqk,cqd->ckd", grad_scores, queries, preferred_element_type=jnp.float32
    ).astype(jnp.bfloat16)
    grad_values = jnp.einsum(
        "cqk,cqd->ckd", probs.astype(jnp.bfloat16), grad_context, preferred_element_type=jnp.float32
    ).astype(jnp.bfloat16)
    return (grad_queries, grad_keys, grad_values)


def body(
    inputs,
    cotangent,
    valid,
    ln1_gain,
    ln1_bias,
    qkv_weight,
    q_bias,
    v_bias,
    out_weight,
    out_bias,
    ln2_gain,
    ln2_bias,
    fc1_weight,
    fc1_bias,
    fc2_weight,
    fc2_bias,
):
    clip_count, row_count, model_width = inputs.shape
    seq_count = lax.axis_size("seq")
    heads_here = HEADS // seq_count
    scale_factor = HEAD ** (-0.5)
    shaped = (clip_count, row_count, model_width)
    key_valid = valid > 0
    full_ln1_gain, full_ln1_bias, full_qkv, full_q_bias, full_v_bias, full_out, full_out_bias = (
        lax.all_gather(ln1_gain, "fsdp", axis=0, tiled=True),
        lax.all_gather(ln1_bias, "fsdp", axis=0, tiled=True),
        lax.all_gather(qkv_weight, "fsdp", axis=0, tiled=True),
        lax.all_gather(q_bias, "fsdp", axis=0, tiled=True),
        lax.all_gather(v_bias, "fsdp", axis=0, tiled=True),
        lax.all_gather(out_weight, "fsdp", axis=0, tiled=True),
        lax.all_gather(out_bias, "fsdp", axis=0, tiled=True),
    )
    residual_in = inputs.reshape(clip_count * row_count, model_width).astype(jnp.float32)
    h_one, norm_one_pull = jax.vjp(
        layer_norm,
        residual_in,
        full_ln1_gain.astype(jnp.float32),
        full_ln1_bias.astype(jnp.float32),
    )
    h_one_low = h_one.astype(jnp.bfloat16)
    mixed = jnp.dot(h_one_low, full_qkv, preferred_element_type=jnp.float32)
    queries = ((mixed[:, :model_width] + full_q_bias.astype(jnp.float32)) * scale_factor).astype(
        jnp.bfloat16
    )
    key_rows = mixed[:, model_width : 2 * model_width].astype(jnp.bfloat16)
    value_rows = (mixed[:, 2 * model_width :] + full_v_bias.astype(jnp.float32)).astype(
        jnp.bfloat16
    )
    query_heads, key_heads, value_heads = (
        lax.all_to_all(queries.reshape(shaped), "seq", split_axis=2, concat_axis=1, tiled=True),
        lax.all_to_all(key_rows.reshape(shaped), "seq", split_axis=2, concat_axis=1, tiled=True),
        lax.all_to_all(value_rows.reshape(shaped), "seq", split_axis=2, concat_axis=1, tiled=True),
    )
    stacked = (
        head_major(query_heads, heads_here),
        head_major(key_heads, heads_here),
        head_major(value_heads, heads_here),
    )
    context_heads, log_totals = lax.map(partial(attend_forward, keep=key_valid), stacked)
    context_tokens = lax.all_to_all(
        token_major(context_heads), "seq", split_axis=1, concat_axis=2, tiled=True
    )
    context_low = context_tokens.reshape(-1, model_width)
    attn_branch = jnp.dot(
        context_low, full_out, preferred_element_type=jnp.float32
    ) + full_out_bias.astype(jnp.float32)
    residual_mid = residual_in + attn_branch
    full_ln2_gain, full_ln2_bias, full_fc1, full_fc1_bias, full_fc2, full_fc2_bias = (
        lax.all_gather(ln2_gain, "fsdp", axis=0, tiled=True),
        lax.all_gather(ln2_bias, "fsdp", axis=0, tiled=True),
        lax.all_gather(fc1_weight, "fsdp", axis=0, tiled=True),
        lax.all_gather(fc1_bias, "fsdp", axis=0, tiled=True),
        lax.all_gather(fc2_weight, "fsdp", axis=0, tiled=True),
        lax.all_gather(fc2_bias, "fsdp", axis=0, tiled=True),
    )
    h_two, norm_two_pull = jax.vjp(
        layer_norm,
        residual_mid,
        full_ln2_gain.astype(jnp.float32),
        full_ln2_bias.astype(jnp.float32),
    )
    h_two_low = h_two.astype(jnp.bfloat16)
    hidden = jnp.dot(
        h_two_low, full_fc1, preferred_element_type=jnp.float32
    ) + full_fc1_bias.astype(jnp.float32)
    active, gelu_pull = jax.vjp(gelu_exact, hidden)
    active_low = active.astype(jnp.bfloat16)
    mlp_branch = jnp.dot(
        active_low, full_fc2, preferred_element_type=jnp.float32
    ) + full_fc2_bias.astype(jnp.float32)
    residual_out = residual_mid + mlp_branch
    own_valid = (
        lax.dynamic_slice_in_dim(valid, lax.axis_index("seq") * row_count, row_count, 1)
        .reshape(-1, 1)
        .astype(jnp.float32)
    )
    totals = lax.psum(
        (
            jnp.sum(own_valid * residual_out * residual_out),
            jnp.sum(own_valid * attn_branch * attn_branch),
            jnp.sum(own_valid * mlp_branch * mlp_branch),
            jnp.sum(own_valid),
        ),
        ("seq", "fsdp"),
    )
    branch_rms = jnp.sqrt(jnp.stack([totals[0], totals[1], totals[2]]) / (totals[3] * model_width))
    full_qkv, full_out, full_fc1, full_fc2 = (
        lax.all_gather(qkv_weight, "fsdp", axis=0, tiled=True),
        lax.all_gather(out_weight, "fsdp", axis=0, tiled=True),
        lax.all_gather(fc1_weight, "fsdp", axis=0, tiled=True),
        lax.all_gather(fc2_weight, "fsdp", axis=0, tiled=True),
    )
    grad_output = cotangent.reshape(-1, model_width)
    grad_fc2_weight = contract_rows(active_low, grad_output)
    grad_fc2_bias = column_sum(grad_output)
    grad_hidden = gelu_pull(times_transpose(grad_output, full_fc2))[0].astype(jnp.bfloat16)
    grad_fc1_weight = contract_rows(h_two_low, grad_hidden)
    grad_fc1_bias = column_sum(grad_hidden)
    grad_mid, grad_ln2_gain, grad_ln2_bias = norm_two_pull(times_transpose(grad_hidden, full_fc1))
    grad_residual = grad_output.astype(jnp.float32) + grad_mid
    grad_attn = grad_residual.astype(jnp.bfloat16)
    grad_out_weight = contract_rows(context_low, grad_attn)
    grad_out_bias = column_sum(grad_attn)
    grad_context = times_transpose(grad_attn, full_out).astype(jnp.bfloat16).reshape(shaped)
    grad_context_heads = lax.all_to_all(
        grad_context, "seq", split_axis=2, concat_axis=1, tiled=True
    )
    grad_query_heads, grad_key_heads, grad_value_heads = lax.map(
        partial(attend_backward, keep=key_valid),
        stacked + (log_totals, head_major(grad_context_heads, heads_here)),
    )
    grad_queries, grad_keys, grad_values = (
        lax.all_to_all(
            token_major(grad_query_heads), "seq", split_axis=1, concat_axis=2, tiled=True
        ),
        lax.all_to_all(token_major(grad_key_heads), "seq", split_axis=1, concat_axis=2, tiled=True),
        lax.all_to_all(
            token_major(grad_value_heads), "seq", split_axis=1, concat_axis=2, tiled=True
        ),
    )
    grad_mixed = jnp.concatenate(
        [
            (grad_queries * scale_factor).reshape(-1, model_width),
            grad_keys.reshape(-1, model_width),
            grad_values.reshape(-1, model_width),
        ],
        axis=1,
    )
    grad_qkv_weight = contract_rows(h_one_low, grad_mixed)
    grad_q_bias = column_sum(grad_mixed[:, :model_width])
    grad_v_bias = column_sum(grad_mixed[:, 2 * model_width :])
    grad_first, grad_ln1_gain, grad_ln1_bias = norm_one_pull(times_transpose(grad_mixed, full_qkv))
    input_grad = (grad_residual + grad_first).astype(jnp.bfloat16).reshape(shaped)
    output = residual_out.astype(jnp.bfloat16).reshape(shaped)
    attn_part = (
        lax.psum_scatter(grad_ln1_gain, "fsdp", scatter_dimension=0, tiled=True),
        lax.psum_scatter(grad_ln1_bias, "fsdp", scatter_dimension=0, tiled=True),
        lax.psum_scatter(grad_qkv_weight, "fsdp", scatter_dimension=0, tiled=True),
        lax.psum_scatter(grad_q_bias, "fsdp", scatter_dimension=0, tiled=True),
        lax.psum_scatter(grad_v_bias, "fsdp", scatter_dimension=0, tiled=True),
        lax.psum_scatter(grad_out_weight, "fsdp", scatter_dimension=0, tiled=True),
        lax.psum_scatter(grad_out_bias, "fsdp", scatter_dimension=0, tiled=True),
    )
    mlp_part = (
        lax.psum_scatter(grad_ln2_gain, "fsdp", scatter_dimension=0, tiled=True),
        lax.psum_scatter(grad_ln2_bias, "fsdp", scatter_dimension=0, tiled=True),
        lax.psum_scatter(grad_fc1_weight, "fsdp", scatter_dimension=0, tiled=True),
        lax.psum_scatter(grad_fc1_bias, "fsdp", scatter_dimension=0, tiled=True),
        lax.psum_scatter(grad_fc2_weight, "fsdp", scatter_dimension=0, tiled=True),
        lax.psum_scatter(grad_fc2_bias, "fsdp", scatter_dimension=0, tiled=True),
    )
    shards = (
        lax.psum(attn_part[0].astype(jnp.bfloat16), "seq").astype(jnp.float32),
        lax.psum(attn_part[1].astype(jnp.bfloat16), "seq").astype(jnp.float32),
        lax.psum(attn_part[2].astype(jnp.bfloat16), "seq").astype(jnp.float32),
        lax.psum(attn_part[3].astype(jnp.bfloat16), "seq").astype(jnp.float32),
        lax.psum(attn_part[4].astype(jnp.bfloat16), "seq").astype(jnp.float32),
        lax.psum(attn_part[5].astype(jnp.bfloat16), "seq").astype(jnp.float32),
        lax.psum(attn_part[6].astype(jnp.bfloat16), "seq").astype(jnp.float32),
        lax.psum(mlp_part[0].astype(jnp.bfloat16), "seq").astype(jnp.float32),
        lax.psum(mlp_part[1].astype(jnp.bfloat16), "seq").astype(jnp.float32),
        lax.psum(mlp_part[2].astype(jnp.bfloat16), "seq").astype(jnp.float32),
        lax.psum(mlp_part[3].astype(jnp.bfloat16), "seq").astype(jnp.float32),
        lax.psum(mlp_part[4].astype(jnp.bfloat16), "seq").astype(jnp.float32),
        lax.psum(mlp_part[5].astype(jnp.bfloat16), "seq").astype(jnp.float32),
    )
    return (
        output,
        input_grad,
        shards[0],
        shards[1],
        shards[2],
        shards[3],
        shards[4],
        shards[5],
        shards[6],
        shards[7],
        shards[8],
        shards[9],
        shards[10],
        shards[11],
        shards[12],
        branch_rms,
    )


def solution(mesh):
    return jax.shard_map(
        body,
        mesh=mesh,
        in_specs=(
            P("fsdp", "seq", None),
            P("fsdp", "seq", None),
            P("fsdp", None),
            P("fsdp"),
            P("fsdp"),
            P("fsdp", None),
            P("fsdp"),
            P("fsdp"),
            P("fsdp", None),
            P("fsdp"),
            P("fsdp"),
            P("fsdp"),
            P("fsdp", None),
            P("fsdp"),
            P("fsdp", None),
            P("fsdp"),
        ),
        out_specs=(
            P("fsdp", "seq", None),
            P("fsdp", "seq", None),
            P("fsdp"),
            P("fsdp"),
            P("fsdp", None),
            P("fsdp"),
            P("fsdp"),
            P("fsdp", None),
            P("fsdp"),
            P("fsdp"),
            P("fsdp"),
            P("fsdp", None),
            P("fsdp"),
            P("fsdp", None),
            P("fsdp"),
            P(),
        ),
        check_vma=False,
    )
```

profile of v0, /device:TPU:0, one launch (start us, length us, event | category | flops | bytes accessed | tf_op | source)
XLA Modules:
  0.0 1738.8 jit_solution(8141717129016121572)
XLA Ops:
  12.0 22.4 %all-gather = bf16[8,1,128]{2,1,0:T(2,128)(2,1)S(1)} all-gather(bf16[1,1,128]{2,1,0:T(2,128)(2,1)S(1)} %bitcast.283), channel_id=1, replica_groups=mesh['seq'=4,'fsdp'=8] {'fsdp'}, dimensions={0}, use_global_device_ids=true | all-gather | bytes 2304 | tf_op jit(solution)/shard_map/all_gather | solution.py:110
  34.4 16.5 all-gather.1
  50.9 18.4 %all-gather.2 = bf16[8,1,128]{2,1,0:T(2,128)(2,1)S(1)} all-gather(bf16[1,1,128]{2,1,0:T(2,128)(2,1)S(1)} %bitcast.285), channel_id=1, replica_groups=mesh['seq'=4,'fsdp'=8] {'fsdp'}, dimensions={0}, use_global_device_ids=true | all-gather | bytes 2304 | tf_op jit(solution)/shard_map/all_gather | solution.py:113
  69.3 16.5 all-gather.3
  86.5 25.7 %all-gather.14.cloned.1.call-done = bf16[1024,3072]{1,0:T(8,128)(2,1)} async-done(((bf16[128,3072]{1,0:T(8,128)(2,1)}), bf16[1024,3072]{1,0:T(8,128)(2,1)}) %all-gather.14.cloned.1.call-update) | async-done | bytes 6291472 | tf_op jit(solution)/shard_map/all_gather | solution.py:112
  137.6 19.5 %all-to-all-done = bf16[2,392,1024]{1,0,2:T(2,128)(2,1)S(1)} async-done(((bf16[2,392,1024]{1,0,2:T(2,128)(2,1)}), bf16[2,392,1024]{1,0,2:T(2,128)(2,1)S(1)}, u32[]{:S(2)}, u32[]{:S(2)}) %all-to-all-start) | async-done | bytes 1605664 | tf_op jit(solution)/shard_map/all_to_all | solution.py:135
  171.0 16.2 all-to-all-done.2
  229.9 58.6 %while.26 = (s32[]{:T(128)}, bf16[4,2,1568,64]{2,3,1,0:T(8,128)(2,1)}, f32[4,2,1568]{2,1,0:T(2,128)}, pred[2,1568]{1,0:T(4,128)(4,1)S(1)}, bf16[4,2,1568,64]{2,3...) while((s32[]{:T(128)}, ...), condition=%wide.region_5.6_spmd, body=%wide.region_2.5_spmd.sunk | while | flops 1303268352 | bytes 60827604 | solution.py:144
  301.6 18.0 %all-gather.4 = bf16[8,1,128]{2,1,0:T(2,128)(2,1)S(1)} all-gather(bf16[1,1,128]{2,1,0:T(2,128)(2,1)S(1)} %bitcast.287), channel_id=1, replica_groups=mesh['seq'=4,'fsdp'=8] {'fsdp'}, dimensions={0}, use_global_device_ids=true | all-gather | bytes 2304 | tf_op jit(solution)/shard_map/all_gather | solution.py:116
  319.7 16.5 all-gather.5
  336.2 18.3 %all-gather.6 = bf16[8,1,128]{2,1,0:T(2,128)(2,1)S(1)} all-gather(bf16[1,1,128]{2,1,0:T(2,128)(2,1)S(1)} %bitcast.289), channel_id=1, replica_groups=mesh['seq'=4,'fsdp'=8] {'fsdp'}, dimensions={0}, use_global_device_ids=true | all-gather | bytes 2304 | tf_op jit(solution)/shard_map/all_gather | solution.py:155
  354.6 26.6 %all-gather.7 = bf16[8,1,512]{2,1,0:T(2,128)(2,1)S(1)} all-gather(bf16[1,1,512]{2,1,0:T(2,128)(2,1)S(1)} %reshape.266), channel_id=1, replica_groups=mesh['seq'=4,'fsdp'=8] {'fsdp'}, dimensions={0}, use_global_device_ids=true | all-gather | bytes 9216 | tf_op jit(solution)/shard_map/all_gather | solution.py:157
  383.2 16.3 all-gather.8
  410.4 13.8 fusion.67
  424.2 40.7 %convert_reduce_fusion = (f32[4096]{0:T(1024)}, bf16[784,4096]{1,0:T(8,128)(2,1)}, f32[784,4096]{1,0:T(8,128)S(1)}) fusion(f32[784,4096]{1,0:T(8,128)} %fusion.67, f32[4096]{0:T(1024)S(1)} %bitcast.262, bf16[784,1024]{1,0:T(8,128)(2,1)} %bitcast.227, bf16[4096,1024]{1,0:T(8,128)(2,1)} %all-gather.20.cloned.1.call-done), kind=kOutput, calls=%fused_computation.56 | convolution fusion | flops 6817509376 | bytes 42139648 | tf_op jit(solution)/shard_map/dot_general | solution.py:30
  512.9 19.3 %all-to-all-done.4 = bf16[2,392,1024]{1,0,2:T(2,128)(2,1)S(1)} async-done(((bf16[2,392,1024]{1,0,2:T(2,128)(2,1)}), bf16[2,392,1024]{1,0,2:T(2,128)(2,1)S(1)}, u32[]{:S(2)}, u32[]{:S(2)}) %all-to-all-start.4) | async-done | bytes 1605664 | tf_op jit(solution)/shard_map/all_to_all | solution.py:210
  544.3 235.7 %while.27 = (s32[]{:T(128)}, bf16[4,2,1568,64]{2,3,1,0:T(8,128)(2,1)}, bf16[4,2,1568,64]{2,3,1,0:T(8,128)(2,1)}, bf16[4,2,1568,64]{2,3,1,0:T(8,128)(2,1)}, pred[...) while((s32[]{:T(128)}, ...), condition=%wide.region_12.13_spmd, body=%wide.region_10.12_spmd.sunk | while | flops 3186975744 | bytes 154863216 | solution.py:213
  555.3 17.3 multiply_reduce_fusion.8
  572.6 14.1 multiply_convert_fusion.3
  614.7 17.1 multiply_reduce_fusion.8
  673.4 17.1 multiply_reduce_fusion.8
  690.5 13.7 multiply_convert_fusion.3
  732.0 17.1 multiply_reduce_fusion.8
  821.8 15.4 all-to-all-done.6
  845.9 15.3 all-to-all-done.7
  877.2 14.8 fusion.66
  893.4 14.7 fusion.76
  912.3 42.8 %all-reduce.9 = (f32[1]{0:T(128)}, f32[1]{0:T(128)}, f32[1]{0:T(128)}, f32[]{:T(128)}) all-reduce(f32[1]{0:T(128)} %bitcast.74, f32[1]{0:T(128)} %bitcast.73, f32[1]{0:T(128)} %bitcast.72, f32[]{:T(128)} %get-tuple-element.252), channel_id=1, replica_groups=mesh['seq'=4,'fsdp'=8] {'seq','fsdp'}, use_global_device_ids=true, to_apply=%region_56.57 | all-reduce | flops 4 | bytes 32 | tf_op jit(solution)/shard_map/psum | solution.py:182
  971.0 110.5 %reduce-scatter.5.cloned.1.call-done = f32[128,3072]{1,0:T(8,128)} async-done(((f32[1024,3072]{1,0:T(8,128)}), f32[128,3072]{1,0:T(8,128)}) %reduce-scatter.5.cloned.1.call-update) | async-done | bytes 1572880 | tf_op jit(solution)/shard_map/reduce_scatter | solution.py:243
  1083.9 283.7 %reduce-scatter.9.cloned.1.call-done = f32[128,4096]{1,0:T(8,128)} async-done(((f32[1024,4096]{1,0:T(8,128)}), f32[128,4096]{1,0:T(8,128)}) %reduce-scatter.9.cloned.1.call-update) | async-done | bytes 2097168 | tf_op jit(solution)/shard_map/reduce_scatter | solution.py:252
  1370.3 283.0 %reduce-scatter.11.cloned.1.call-done = f32[512,1024]{1,0:T(8,128)} async-done(((f32[4096,1024]{1,0:T(8,128)}), f32[512,1024]{1,0:T(8,128)}) %reduce-scatter.11.cloned.1.call-update) | async-done | bytes 2097168 | tf_op jit(solution)/shard_map/reduce_scatter | solution.py:254
  1659.1 35.7 %all-reduce.10 = (bf16[1024]{0:T(1024)(128)(2,1)S(1)}, bf16[1024]{0:T(1024)(128)(2,1)S(1)}, bf16[1024]{0:T(1024)(128)(2,1)S(1)}, bf16[1024]{0:T(1024)(128)(2,1)S...) all-reduce(f32[1024]{0:T(1024)S(1)} %get-tuple-element.185, ...), channel_id=2, replica_groups=mesh['seq'=4,'fsdp'=8] {'fsdp'}, use_global_device_ids=true, to_apply=%region_16.17.clone | all-reduce | flops 12288 | bytes 73728
  (346 shorter events, 504.8 us)
Async XLA Ops:
  7.2 62.0 %copy-start.66 = (bf16[128]{0:T(256)(128)(2,1)S(1)}, bf16[128]{0:T(256)(128)(2,1)}, u32[]{:S(2)}) copy-start(bf16[128]{0:T(256)(128)(2,1)} %param.27) | copy-start | bytes 772
  7.2 104.9 %all-gather.14.cloned.1.call-start = ((), (), s32[]{:S(2)}) async-start(), calls=%async_computation.12 | async-start | bytes 7077888 | tf_op jit(solution)/shard_map/all_gather | solution.py:112
  8.0 394.5 %all-gather.16.cloned.1.call-start = ((), (), s32[]{:S(2)}) async-start(), calls=%async_computation.13 | async-start | bytes 2359296 | tf_op jit(solution)/shard_map/all_gather | solution.py:115
  8.7 400.6 %all-gather.18.cloned.1.call-start = ((), (), s32[]{:S(2)}) async-start(), calls=%async_computation.14 | async-start | bytes 9437184 | tf_op jit(solution)/shard_map/all_gather | solution.py:156
  11.3 108.1 %copy-start.30 = (f32[784]{0:T(1024)}, f32[784]{0:T(1024)S(1)}, u32[]{:S(2)}) copy-start(f32[784]{0:T(1024)S(1)} %div.53) | copy-start | bytes 9412
  11.9 73.8 %copy-start.43 = (f32[784]{0:T(1024)}, f32[784]{0:T(1024)S(1)}, u32[]{:S(2)}) copy-start(f32[784]{0:T(1024)S(1)} %add.176) | copy-start | bytes 9412
  11.9 73.8 %copy-start.32 = (f32[784]{0:T(1024)}, f32[784]{0:T(1024)S(1)}, u32[]{:S(2)}) copy-start(f32[784]{0:T(1024)S(1)} %rsqrt.20) | copy-start | bytes 9412
  34.4 51.4 %copy-start.34 = (f32[8,1,128]{2,1,0:T(1,128)}, f32[8,1,128]{2,1,0:T(1,128)S(1)}, u32[]{:S(2)}) copy-start(f32[8,1,128]{2,1,0:T(1,128)S(1)} %convert_element_type.259) | copy-start | bytes 12292
  127.7 29.3 %all-to-all-start = ((bf16[2,392,1024]{1,0,2:T(2,128)(2,1)}), bf16[2,392,1024]{1,0,2:T(2,128)(2,1)S(1)}, u32[]{:S(2)}, u32[]{:S(2)}) async-start(bf16[2,392,1024]{1,0,2:T(2,128)(2,1)} %copy.128), calls=%async_computation | async-start | bytes 4194304 | tf_op jit(solution)/shard_map/all_to_all | solution.py:135
  157.0 30.2 %all-to-all-start.2 = ((bf16[2,392,1024]{1,0,2:T(2,128)(2,1)}), bf16[2,392,1024]{1,0,2:T(2,128)(2,1)}, u32[]{:S(2)}, u32[]{:S(2)}) async-start(bf16[2,392,1024]{1,0,2:T(2,128)(2,1)} %copy.134), calls=%async_computation.2 | async-start | bytes 4194304 | tf_op jit(solution)/shard_map/all_to_all | solution.py:137
  187.3 30.2 %all-to-all-start.1 = ((bf16[2,392,1024]{1,0,2:T(2,128)(2,1)}), bf16[2,392,1024]{1,0,2:T(2,128)(2,1)}, u32[]{:S(2)}, u32[]{:S(2)}) async-start(bf16[2,392,1024]{1,0,2:T(2,128)(2,1)} %copy.131), calls=%async_computation.1 | async-start | bytes 4194304 | tf_op jit(solution)/shard_map/all_to_all | solution.py:136
  191.7 232.5 %all-gather.20.cloned.1.call-start = ((), (), s32[]{:S(2)}) async-start(), calls=%async_computation.15 | async-start | bytes 9437184 | tf_op jit(solution)/shard_map/all_gather | solution.py:158
  288.5 114.0 %copy-start.2 = (bf16[4,2,1568,64]{2,3,1,0:T(8,128)(2,1)}, bf16[4,2,1568,64]{2,3,1,0:T(8,128)(2,1)S(1)}, u32[]{:S(2)}) copy-start(bf16[4,2,1568,64]{2,3,1,0:T(8,128)(2,1)S(1)} %get-tuple-element.457) | copy-start | bytes 4816900
  292.5 62.0 %copy-start.62 = (bf16[512]{0:T(512)(128)(2,1)S(1)}, bf16[512]{0:T(512)(128)(2,1)}, u32[]{:S(2)}) copy-start(bf16[512]{0:T(512)(128)(2,1)} %param.33) | copy-start | bytes 3076
  292.5 90.7 %copy-start.70 = (bf16[128]{0:T(256)(128)(2,1)S(1)}, bf16[128]{0:T(256)(128)(2,1)}, u32[]{:S(2)}) copy-start(bf16[128]{0:T(256)(128)(2,1)} %param.35) | copy-start | bytes 772
  298.1 102.0 %all-to-all-start.3 = ((bf16[2,1568,256]{2,0,1:T(2,128)(2,1)}), bf16[2,1568,256]{2,0,1:T(2,128)(2,1)S(1)}, u32[]{:S(2)}, u32[]{:S(2)}) async-start(bf16[2,1568,256]{2,0,1:T(2,128)(2,1)} %copy.141), calls=%async_computation.3 | async-start | bytes 3211264 | tf_op jit(solution)/shard_map/all_to_all | solution.py:145
  319.7 82.8 %copy-start.58 = (f32[8,1,128]{2,1,0:T(1,128)}, f32[8,1,128]{2,1,0:T(1,128)S(1)}, u32[]{:S(2)}) copy-start(f32[8,1,128]{2,1,0:T(1,128)S(1)} %convert_element_type.263) | copy-start | bytes 12292
  336.2 73.1 %copy-start.47 = (f32[8,1,128]{2,1,0:T(1,128)}, f32[8,1,128]{2,1,0:T(1,128)S(1)}, u32[]{:S(2)}) copy-start(f32[8,1,128]{2,1,0:T(1,128)S(1)} %convert_element_type.264) | copy-start | bytes 12292
  354.5 54.8 %copy-start.56 = (f32[8,1,128]{2,1,0:T(1,128)}, f32[8,1,128]{2,1,0:T(1,128)S(1)}, u32[]{:S(2)}) copy-start(f32[8,1,128]{2,1,0:T(1,128)S(1)} %convert_element_type.265) | copy-start | bytes 12292
  503.0 29.3 %all-to-all-start.4 = ((bf16[2,392,1024]{1,0,2:T(2,128)(2,1)}), bf16[2,392,1024]{1,0,2:T(2,128)(2,1)S(1)}, u32[]{:S(2)}, u32[]{:S(2)}) async-start(bf16[2,392,1024]{1,0,2:T(2,128)(2,1)} %copy.144), calls=%async_computation.4 | async-start | bytes 4194304 | tf_op jit(solution)/shard_map/all_to_all | solution.py:210
  506.6 462.7 %reduce-scatter.7.cloned.1.call-start = ((), (), s32[]{:S(2)}) async-start(), calls=%async_computation.17 | async-start | bytes 4718592 | tf_op jit(solution)/shard_map/reduce_scatter | solution.py:246
  788.2 24.2 %all-to-all-start.5 = ((bf16[2,1568,256]{2,0,1:T(2,128)(2,1)}), bf16[2,1568,256]{2,0,1:T(2,128)(2,1)S(1)}, u32[]{:S(2)}, u32[]{:S(2)}) async-start(bf16[2,1568,256]{2,0,1:T(2,128)(2,1)} %copy.152), calls=%async_computation.5 | async-start | bytes 3211264 | tf_op jit(solution)/shard_map/all_to_all | solution.py:218
  812.4 24.9 %all-to-all-start.6 = ((bf16[2,1568,256]{2,0,1:T(2,128)(2,1)}), bf16[2,1568,256]{2,0,1:T(2,128)(2,1)}, u32[]{:S(2)}, u32[]{:S(2)}) async-start(bf16[2,1568,256]{2,0,1:T(2,128)(2,1)} %copy.156), calls=%async_computation.6 | async-start | bytes 3211264 | tf_op jit(solution)/shard_map/all_to_all | solution.py:221
  837.2 24.0 %all-to-all-start.7 = ((bf16[2,1568,256]{2,0,1:T(2,128)(2,1)}), bf16[2,1568,256]{2,0,1:T(2,128)(2,1)S(1)}, u32[]{:S(2)}, u32[]{:S(2)}) async-start(bf16[2,1568,256]{2,0,1:T(2,128)(2,1)} %copy.160), calls=%async_computation.7 | async-start | bytes 3211264 | tf_op jit(solution)/shard_map/all_to_all | solution.py:222
  840.8 240.7 %reduce-scatter.5.cloned.1.call-start = ((), (), s32[]{:S(2)}) async-start(), calls=%async_computation.16 | async-start | bytes 14155776 | tf_op jit(solution)/shard_map/reduce_scatter | solution.py:243
  875.3 492.3 %reduce-scatter.9.cloned.1.call-start = ((), (), s32[]{:S(2)}) async-start(), calls=%async_computation.18 | async-start | bytes 18874368 | tf_op jit(solution)/shard_map/reduce_scatter | solution.py:252
  892.0 761.3 %reduce-scatter.11.cloned.1.call-start = ((), (), s32[]{:S(2)}) async-start(), calls=%async_computation.19 | async-start | bytes 18874368 | tf_op jit(solution)/shard_map/reduce_scatter | solution.py:254
  908.1 50.4 %copy-start.9 = (bf16[2,392,1024]{2,1,0:T(8,128)(2,1)S(1)}, bf16[2,392,1024]{2,1,0:T(8,128)(2,1)}, u32[]{:S(2)}) copy-start(bf16[2,392,1024]{2,1,0:T(8,128)(2,1)} %param.20) | copy-start | bytes 4816900
  908.1 50.4 %copy-start.31 = (f32[784]{0:T(1024)S(1)}, f32[784]{0:T(1024)}, u32[]{:S(2)}) copy-start(f32[784]{0:T(1024)} %copy-done.30) | copy-start | bytes 9412
  908.1 817.3 %all-reduce.15.cloned.1.call-start = ((), (), s32[]{:S(2)}) async-start(), calls=%async_computation.20 | async-start | bytes 6291456 | tf_op jit(solution)/shard_map/psum | solution.py:260
  1370.3 285.7 %copy-start.11 = (bf16[2,1568,256]{2,0,1:T(2,128)(2,1)S(1)}, bf16[2,1568,256]{2,0,1:T(2,128)(2,1)}, u32[]{:S(2)}) copy-start(bf16[2,1568,256]{2,0,1:T(2,128)(2,1)} %copy-done.10) | copy-start | bytes 4816900
  1656.0 50.6 %copy-start.44 = (f32[784]{0:T(1024)S(1)}, f32[784]{0:T(1024)}, u32[]{:S(2)}) copy-start(f32[784]{0:T(1024)} %copy-done.43) | copy-start | bytes 9412
  (60 other events, 710.4 us)
Sparse Core Ops, SparseCore 0:
  10.2 101.8 all-gather.13
  114.3 47.4 all-gather.15
  164.0 123.4 all-gather.17
  289.4 123.5 all-gather.19
  513.0 87.4 reduce-scatter.6
  875.4 206.0 reduce-scatter.4
  1085.8 281.7 reduce-scatter.8
  1371.4 281.8 reduce-scatter.10
  1657.2 68.2 all-reduce.14
where the time goes:
time: 1750 us; the launch traced here: 1740 us
  waiting for transfers between devices  820 us (47%)
  matrix products  365 us (21%)
  blocking collectives  254 us (15%)
  other arithmetic  130 us (7%)
  local copies, waits for them, and re-layouts  120 us (7%)
  starting transfers between devices  32.3 us (2%)
    reduce_scatter x1, waiting for transfers between devices, body(): lax.psum_scatter(grad_fc1_weight, 'fsdp', scatter_dimension=0, tiled=True)  284 us
    reduce_scatter x1, waiting for transfers between devices, body(): lax.psum_scatter(grad_fc2_weight, 'fsdp', scatter_dimension=0, tiled=True)  283 us
    reduce_scatter x1, waiting for transfers between devices, body(): lax.psum_scatter(grad_qkv_weight, 'fsdp', scatter_dimension=0, tiled=True)  110 us
    dot_general x4, matrix products, attend_backward(): jnp.einsum('cqd,ckd->cqk', grad_context, value_rows, preferred_element_ty...  68.7 us
    dot_general x4, matrix products, times_transpose(): lax.dot_general(left, right, (((1,), (1,)), ((), ())), preferred_element_...  64.5 us
    convert_element_type x4, other arithmetic, attend_backward(): grad_scores = (probs * (grad_probs - inner)).astype(jnp.bfloat16)  55.1 us
    dot_general x4, matrix products, contract_rows(): lax.dot_general(left, right, (((0,), (0,)), ((), ())), preferred_element_...  45.1 us
    psum x1, blocking collectives, body(): lax.psum((jnp.sum(own_valid * residual_out * residual_out), jnp.sum(own_v...  42.8 us
  transfers between devices with their start and end apart: 17, of which 12 were waited for; matrix products, arithmetic and copies ran while one was open for 30% of the time, Pallas kernels for 0%

commit v1 on v0

--- a/solution.py
+++ b/solution.py
@@ -180,13 +180,16 @@
         .astype(jnp.float32)
     )
     totals = lax.psum(
-        (
-            jnp.sum(own_valid * residual_out * residual_out),
-            jnp.sum(own_valid * attn_branch * attn_branch),
-            jnp.sum(own_valid * mlp_branch * mlp_branch),
-            jnp.sum(own_valid),
-        ),
-        ("seq", "fsdp"),
+        lax.psum(
+            (
+                jnp.sum(own_valid * residual_out * residual_out),
+                jnp.sum(own_valid * attn_branch * attn_branch),
+                jnp.sum(own_valid * mlp_branch * mlp_branch),
+                jnp.sum(own_valid),
+            ),
+            "seq",
+        ),
+        "fsdp",
     )
     branch_rms = jnp.sqrt(jnp.stack([totals[0], totals[1], totals[2]]) / (totals[3] * model_width))
     full_qkv, full_out, full_fc1, full_fc2 = (

time: 1750 us -> 1750 us (level)
  blocking collectives: 254 us -> 218 us
  waiting for transfers between devices: 820 us -> 856 us
    reduce_scatter x1, waiting for transfers between devices: 110 us -> 148 us  [body(): lax.psum_scatter(grad_qkv_weight, 'fsdp', scatter_dimension=0, tiled=True)]
    psum x1, blocking collectives: 42.8 us -> 6.71 us  [body(): lax.psum((jnp.sum(own_valid * residual_out * residual_out), jnp.sum(own_v...]
where the time goes in v1:
time: 1750 us; the launch traced here: 1740 us
  waiting for transfers between devices  856 us (49%)
  matrix products  365 us (21%)
  blocking collectives  218 us (12%)
  other arithmetic  130 us (7%)
  local copies, waits for them, and re-layouts  120 us (7%)
  starting transfers between devices  32.2 us (2%)
    reduce_scatter x1, waiting for transfers between devices, body(): lax.psum_scatter(grad_fc1_weight, 'fsdp', scatter_dimension=0, tiled=True)  284 us
    reduce_scatter x1, waiting for transfers between devices, body(): lax.psum_scatter(grad_fc2_weight, 'fsdp', scatter_dimension=0, tiled=True)  283 us
    reduce_scatter x1, waiting for transfers between devices, body(): lax.psum_scatter(grad_qkv_weight, 'fsdp', scatter_dimension=0, tiled=True)  148 us
    dot_general x4, matrix products, attend_backward(): jnp.einsum('cqd,ckd->cqk', grad_context, value_rows, preferred_element_ty...  68.7 us
    dot_general x4, matrix products, times_transpose(): lax.dot_general(left, right, (((1,), (1,)), ((), ())), preferred_element_...  64.5 us
    convert_element_type x4, other arithmetic, attend_backward(): grad_scores = (probs * (grad_probs - inner)).astype(jnp.bfloat16)  55.1 us
    dot_general x4, matrix products, contract_rows(): lax.dot_general(left, right, (((0,), (0,)), ((), ())), preferred_element_...  44.9 us
    dot_general x4, matrix products, attend_backward(): jnp.einsum('cqd,ckd->cqk', queries, key_rows, preferred_element_type=jnp....  40.7 us
  transfers between devices with their start and end apart: 17, of which 12 were waited for; matrix products, arithmetic and copies ran while one was open for 30% of the time, Pallas kernels for 0%

profile of v1, /device:TPU:0, one launch (start us, length us, event | category | flops | bytes accessed | tf_op | source)
XLA Modules:
  0.0 1738.0 jit_solution(11855731812495855105)
XLA Ops:
  12.0 22.4 %all-gather = bf16[8,1,128]{2,1,0:T(2,128)(2,1)S(1)} all-gather(bf16[1,1,128]{2,1,0:T(2,128)(2,1)S(1)} %bitcast.283), channel_id=1, replica_groups=mesh['seq'=4,'fsdp'=8] {'fsdp'}, dimensions={0}, use_global_device_ids=true | all-gather | bytes 2304 | tf_op jit(solution)/shard_map/all_gather | solution.py:110
  34.4 16.5 all-gather.1
  50.9 18.4 %all-gather.2 = bf16[8,1,128]{2,1,0:T(2,128)(2,1)S(1)} all-gather(bf16[1,1,128]{2,1,0:T(2,128)(2,1)S(1)} %bitcast.285), channel_id=1, replica_groups=mesh['seq'=4,'fsdp'=8] {'fsdp'}, dimensions={0}, use_global_device_ids=true | all-gather | bytes 2304 | tf_op jit(solution)/shard_map/all_gather | solution.py:113
  69.3 16.5 all-gather.3
  86.5 25.7 %all-gather.14.cloned.1.call-done = bf16[1024,3072]{1,0:T(8,128)(2,1)} async-done(((bf16[128,3072]{1,0:T(8,128)(2,1)}), bf16[1024,3072]{1,0:T(8,128)(2,1)}) %all-gather.14.cloned.1.call-update) | async-done | bytes 6291472 | tf_op jit(solution)/shard_map/all_gather | solution.py:112
  137.6 19.5 %all-to-all-done = bf16[2,392,1024]{1,0,2:T(2,128)(2,1)S(1)} async-done(((bf16[2,392,1024]{1,0,2:T(2,128)(2,1)}), bf16[2,392,1024]{1,0,2:T(2,128)(2,1)S(1)}, u32[]{:S(2)}, u32[]{:S(2)}) %all-to-all-start) | async-done | bytes 1605664 | tf_op jit(solution)/shard_map/all_to_all | solution.py:135
  171.0 16.2 all-to-all-done.2
  229.9 58.6 %while.26 = (s32[]{:T(128)}, bf16[4,2,1568,64]{2,3,1,0:T(8,128)(2,1)}, f32[4,2,1568]{2,1,0:T(2,128)}, pred[2,1568]{1,0:T(4,128)(4,1)S(1)}, bf16[4,2,1568,64]{2,3...) while((s32[]{:T(128)}, ...), condition=%wide.region_5.6_spmd, body=%wide.region_2.5_spmd.sunk | while | flops 1303268352 | bytes 60827604 | solution.py:144
  301.7 18.0 %all-gather.4 = bf16[8,1,128]{2,1,0:T(2,128)(2,1)S(1)} all-gather(bf16[1,1,128]{2,1,0:T(2,128)(2,1)S(1)} %bitcast.287), channel_id=1, replica_groups=mesh['seq'=4,'fsdp'=8] {'fsdp'}, dimensions={0}, use_global_device_ids=true | all-gather | bytes 2304 | tf_op jit(solution)/shard_map/all_gather | solution.py:116
  319.7 16.5 all-gather.5
  336.2 18.3 %all-gather.6 = bf16[8,1,128]{2,1,0:T(2,128)(2,1)S(1)} all-gather(bf16[1,1,128]{2,1,0:T(2,128)(2,1)S(1)} %bitcast.289), channel_id=1, replica_groups=mesh['seq'=4,'fsdp'=8] {'fsdp'}, dimensions={0}, use_global_device_ids=true | all-gather | bytes 2304 | tf_op jit(solution)/shard_map/all_gather | solution.py:155
  354.6 26.6 %all-gather.7 = bf16[8,1,512]{2,1,0:T(2,128)(2,1)S(1)} all-gather(bf16[1,1,512]{2,1,0:T(2,128)(2,1)S(1)} %reshape.266), channel_id=1, replica_groups=mesh['seq'=4,'fsdp'=8] {'fsdp'}, dimensions={0}, use_global_device_ids=true | all-gather | bytes 9216 | tf_op jit(solution)/shard_map/all_gather | solution.py:157
  383.2 16.3 all-gather.8
  410.4 13.8 fusion.67
  424.2 40.7 %convert_reduce_fusion = (f32[4096]{0:T(1024)}, bf16[784,4096]{1,0:T(8,128)(2,1)}, f32[784,4096]{1,0:T(8,128)S(1)}) fusion(f32[784,4096]{1,0:T(8,128)} %fusion.67, f32[4096]{0:T(1024)S(1)} %bitcast.262, bf16[784,1024]{1,0:T(8,128)(2,1)} %bitcast.227, bf16[4096,1024]{1,0:T(8,128)(2,1)} %all-gather.20.cloned.1.call-done), kind=kOutput, calls=%fused_computation.56 | convolution fusion | flops 6817509376 | bytes 42139648 | tf_op jit(solution)/shard_map/dot_general | solution.py:30
  512.9 19.3 %all-to-all-done.4 = bf16[2,392,1024]{1,0,2:T(2,128)(2,1)S(1)} async-done(((bf16[2,392,1024]{1,0,2:T(2,128)(2,1)}), bf16[2,392,1024]{1,0,2:T(2,128)(2,1)S(1)}, u32[]{:S(2)}, u32[]{:S(2)}) %all-to-all-start.4) | async-done | bytes 1605664 | tf_op jit(solution)/shard_map/all_to_all | solution.py:213
  544.2 235.7 %while.27 = (s32[]{:T(128)}, bf16[4,2,1568,64]{2,3,1,0:T(8,128)(2,1)}, bf16[4,2,1568,64]{2,3,1,0:T(8,128)(2,1)}, bf16[4,2,1568,64]{2,3,1,0:T(8,128)(2,1)}, pred[...) while((s32[]{:T(128)}, ...), condition=%wide.region_12.13_spmd, body=%wide.region_10.12_spmd.sunk | while | flops 3186975744 | bytes 154863216 | solution.py:216
  555.3 17.3 multiply_reduce_fusion.8
  572.6 14.1 multiply_convert_fusion.3
  614.7 17.1 multiply_reduce_fusion.8
  631.8 13.7 multiply_convert_fusion.3
  673.3 17.1 multiply_reduce_fusion.8
  690.5 13.7 multiply_convert_fusion.3
  732.0 17.1 multiply_reduce_fusion.8
  821.8 15.4 all-to-all-done.6
  845.9 15.3 all-to-all-done.7
  877.1 14.8 fusion.66
  893.4 14.6 fusion.76
  932.9 147.7 %reduce-scatter.5.cloned.1.call-done = f32[128,3072]{1,0:T(8,128)} async-done(((f32[1024,3072]{1,0:T(8,128)}), f32[128,3072]{1,0:T(8,128)}) %reduce-scatter.5.cloned.1.call-update) | async-done | bytes 1572880 | tf_op jit(solution)/shard_map/reduce_scatter | solution.py:246
  1083.1 283.7 %reduce-scatter.9.cloned.1.call-done = f32[128,4096]{1,0:T(8,128)} async-done(((f32[1024,4096]{1,0:T(8,128)}), f32[128,4096]{1,0:T(8,128)}) %reduce-scatter.9.cloned.1.call-update) | async-done | bytes 2097168 | tf_op jit(solution)/shard_map/reduce_scatter | solution.py:255
  1369.5 282.8 %reduce-scatter.11.cloned.1.call-done = f32[512,1024]{1,0:T(8,128)} async-done(((f32[4096,1024]{1,0:T(8,128)}), f32[512,1024]{1,0:T(8,128)}) %reduce-scatter.11.cloned.1.call-update) | async-done | bytes 2097168 | tf_op jit(solution)/shard_map/reduce_scatter | solution.py:257
  1656.8 35.8 %all-reduce.9 = (bf16[1024]{0:T(1024)(128)(2,1)S(1)}, bf16[1024]{0:T(1024)(128)(2,1)S(1)}, bf16[1024]{0:T(1024)(128)(2,1)S(1)}, bf16[1024]{0:T(1024)(128)(2,1)S(...) all-reduce(f32[1024]{0:T(1024)S(1)} %get-tuple-element.185, ...), channel_id=2, replica_groups=mesh['seq'=4,'fsdp'=8] {'fsdp'}, use_global_device_ids=true, to_apply=%region_16.17.clone | all-reduce | flops 12292 | bytes 73760
  (346 shorter events, 495.9 us)
Async XLA Ops:
  7.2 43.6 %copy-start.65 = (bf16[128]{0:T(256)(128)(2,1)S(1)}, bf16[128]{0:T(256)(128)(2,1)}, u32[]{:S(2)}) copy-start(bf16[128]{0:T(256)(128)(2,1)} %param.26) | copy-start | bytes 772
  7.2 62.0 %copy-start.66 = (bf16[128]{0:T(256)(128)(2,1)S(1)}, bf16[128]{0:T(256)(128)(2,1)}, u32[]{:S(2)}) copy-start(bf16[128]{0:T(256)(128)(2,1)} %param.27) | copy-start | bytes 772
  7.2 104.9 %all-gather.14.cloned.1.call-start = ((), (), s32[]{:S(2)}) async-start(), calls=%async_computation.12 | async-start | bytes 7077888 | tf_op jit(solution)/shard_map/all_gather | solution.py:112
  8.0 394.5 %all-gather.16.cloned.1.call-start = ((), (), s32[]{:S(2)}) async-start(), calls=%async_computation.13 | async-start | bytes 2359296 | tf_op jit(solution)/shard_map/all_gather | solution.py:115
  8.7 400.6 %all-gather.18.cloned.1.call-start = ((), (), s32[]{:S(2)}) async-start(), calls=%async_computation.14 | async-start | bytes 9437184 | tf_op jit(solution)/shard_map/all_gather | solution.py:156
  11.3 108.1 %copy-start.30 = (f32[784]{0:T(1024)}, f32[784]{0:T(1024)S(1)}, u32[]{:S(2)}) copy-start(f32[784]{0:T(1024)S(1)} %div.53) | copy-start | bytes 9412
  11.9 73.8 %copy-start.43 = (f32[784]{0:T(1024)}, f32[784]{0:T(1024)S(1)}, u32[]{:S(2)}) copy-start(f32[784]{0:T(1024)S(1)} %add.184) | copy-start | bytes 9412
  11.9 73.8 %copy-start.32 = (f32[784]{0:T(1024)}, f32[784]{0:T(1024)S(1)}, u32[]{:S(2)}) copy-start(f32[784]{0:T(1024)S(1)} %rsqrt.20) | copy-start | bytes 9412
  34.4 51.4 %copy-start.34 = (f32[8,1,128]{2,1,0:T(1,128)}, f32[8,1,128]{2,1,0:T(1,128)S(1)}, u32[]{:S(2)}) copy-start(f32[8,1,128]{2,1,0:T(1,128)S(1)} %convert_element_type.259) | copy-start | bytes 12292
  127.8 29.3 %all-to-all-start = ((bf16[2,392,1024]{1,0,2:T(2,128)(2,1)}), bf16[2,392,1024]{1,0,2:T(2,128)(2,1)S(1)}, u32[]{:S(2)}, u32[]{:S(2)}) async-start(bf16[2,392,1024]{1,0,2:T(2,128)(2,1)} %copy.128), calls=%async_computation | async-start | bytes 4194304 | tf_op jit(solution)/shard_map/all_to_all | solution.py:135
  157.0 30.2 %all-to-all-start.2 = ((bf16[2,392,1024]{1,0,2:T(2,128)(2,1)}), bf16[2,392,1024]{1,0,2:T(2,128)(2,1)}, u32[]{:S(2)}, u32[]{:S(2)}) async-start(bf16[2,392,1024]{1,0,2:T(2,128)(2,1)} %copy.134), calls=%async_computation.2 | async-start | bytes 4194304 | tf_op jit(solution)/shard_map/all_to_all | solution.py:137
  187.3 30.2 %all-to-all-start.1 = ((bf16[2,392,1024]{1,0,2:T(2,128)(2,1)}), bf16[2,392,1024]{1,0,2:T(2,128)(2,1)}, u32[]{:S(2)}, u32[]{:S(2)}) async-start(bf16[2,392,1024]{1,0,2:T(2,128)(2,1)} %copy.131), calls=%async_computation.1 | async-start | bytes 4194304 | tf_op jit(solution)/shard_map/all_to_all | solution.py:136
  191.7 232.4 %all-gather.20.cloned.1.call-start = ((), (), s32[]{:S(2)}) async-start(), calls=%async_computation.15 | async-start | bytes 9437184 | tf_op jit(solution)/shard_map/all_gather | solution.py:158
  288.5 113.9 %copy-start.2 = (bf16[4,2,1568,64]{2,3,1,0:T(8,128)(2,1)}, bf16[4,2,1568,64]{2,3,1,0:T(8,128)(2,1)S(1)}, u32[]{:S(2)}) copy-start(bf16[4,2,1568,64]{2,3,1,0:T(8,128)(2,1)S(1)} %get-tuple-element.461) | copy-start | bytes 4816900
  292.5 43.7 %copy-start.69 = (bf16[128]{0:T(256)(128)(2,1)S(1)}, bf16[128]{0:T(256)(128)(2,1)}, u32[]{:S(2)}) copy-start(bf16[128]{0:T(256)(128)(2,1)} %param.31) | copy-start | bytes 772
  292.5 62.0 %copy-start.62 = (bf16[512]{0:T(512)(128)(2,1)S(1)}, bf16[512]{0:T(512)(128)(2,1)}, u32[]{:S(2)}) copy-start(bf16[512]{0:T(512)(128)(2,1)} %param.33) | copy-start | bytes 3076
  292.5 90.7 %copy-start.70 = (bf16[128]{0:T(256)(128)(2,1)S(1)}, bf16[128]{0:T(256)(128)(2,1)}, u32[]{:S(2)}) copy-start(bf16[128]{0:T(256)(128)(2,1)} %param.35) | copy-start | bytes 772
  298.1 102.0 %all-to-all-start.3 = ((bf16[2,1568,256]{2,0,1:T(2,128)(2,1)}), bf16[2,1568,256]{2,0,1:T(2,128)(2,1)S(1)}, u32[]{:S(2)}, u32[]{:S(2)}) async-start(bf16[2,1568,256]{2,0,1:T(2,128)(2,1)} %copy.141), calls=%async_computation.3 | async-start | bytes 3211264 | tf_op jit(solution)/shard_map/all_to_all | solution.py:145
  319.7 82.7 %copy-start.58 = (f32[8,1,128]{2,1,0:T(1,128)}, f32[8,1,128]{2,1,0:T(1,128)S(1)}, u32[]{:S(2)}) copy-start(f32[8,1,128]{2,1,0:T(1,128)S(1)} %convert_element_type.263) | copy-start | bytes 12292
  336.2 73.1 %copy-start.47 = (f32[8,1,128]{2,1,0:T(1,128)}, f32[8,1,128]{2,1,0:T(1,128)S(1)}, u32[]{:S(2)}) copy-start(f32[8,1,128]{2,1,0:T(1,128)S(1)} %convert_element_type.264) | copy-start | bytes 12292
  354.5 54.8 %copy-start.56 = (f32[8,1,128]{2,1,0:T(1,128)}, f32[8,1,128]{2,1,0:T(1,128)S(1)}, u32[]{:S(2)}) copy-start(f32[8,1,128]{2,1,0:T(1,128)S(1)} %convert_element_type.265) | copy-start | bytes 12292
  502.9 29.3 %all-to-all-start.4 = ((bf16[2,392,1024]{1,0,2:T(2,128)(2,1)}), bf16[2,392,1024]{1,0,2:T(2,128)(2,1)S(1)}, u32[]{:S(2)}, u32[]{:S(2)}) async-start(bf16[2,392,1024]{1,0,2:T(2,128)(2,1)} %copy.144), calls=%async_computation.4 | async-start | bytes 4194304 | tf_op jit(solution)/shard_map/all_to_all | solution.py:213
  506.5 424.6 %reduce-scatter.7.cloned.1.call-start = ((), (), s32[]{:S(2)}) async-start(), calls=%async_computation.17 | async-start | bytes 4718592 | tf_op jit(solution)/shard_map/reduce_scatter | solution.py:249
  788.2 24.2 %all-to-all-start.5 = ((bf16[2,1568,256]{2,0,1:T(2,128)(2,1)}), bf16[2,1568,256]{2,0,1:T(2,128)(2,1)S(1)}, u32[]{:S(2)}, u32[]{:S(2)}) async-start(bf16[2,1568,256]{2,0,1:T(2,128)(2,1)} %copy.152), calls=%async_computation.5 | async-start | bytes 3211264 | tf_op jit(solution)/shard_map/all_to_all | solution.py:221
  812.4 24.9 %all-to-all-start.6 = ((bf16[2,1568,256]{2,0,1:T(2,128)(2,1)}), bf16[2,1568,256]{2,0,1:T(2,128)(2,1)}, u32[]{:S(2)}, u32[]{:S(2)}) async-start(bf16[2,1568,256]{2,0,1:T(2,128)(2,1)} %copy.156), calls=%async_computation.6 | async-start | bytes 3211264 | tf_op jit(solution)/shard_map/all_to_all | solution.py:224
  837.2 24.0 %all-to-all-start.7 = ((bf16[2,1568,256]{2,0,1:T(2,128)(2,1)}), bf16[2,1568,256]{2,0,1:T(2,128)(2,1)S(1)}, u32[]{:S(2)}, u32[]{:S(2)}) async-start(bf16[2,1568,256]{2,0,1:T(2,128)(2,1)} %copy.160), calls=%async_computation.7 | async-start | bytes 3211264 | tf_op jit(solution)/shard_map/all_to_all | solution.py:225
  840.8 239.9 %reduce-scatter.5.cloned.1.call-start = ((), (), s32[]{:S(2)}) async-start(), calls=%async_computation.16 | async-start | bytes 14155776 | tf_op jit(solution)/shard_map/reduce_scatter | solution.py:246
  875.3 491.5 %reduce-scatter.9.cloned.1.call-start = ((), (), s32[]{:S(2)}) async-start(), calls=%async_computation.18 | async-start | bytes 18874368 | tf_op jit(solution)/shard_map/reduce_scatter | solution.py:255
  892.0 760.3 %reduce-scatter.11.cloned.1.call-start = ((), (), s32[]{:S(2)}) async-start(), calls=%async_computation.19 | async-start | bytes 18874368 | tf_op jit(solution)/shard_map/reduce_scatter | solution.py:257
  908.0 816.4 %all-reduce.15.cloned.1.call-start = ((), (), s32[]{:S(2)}) async-start(), calls=%async_computation.20 | async-start | bytes 6291456 | tf_op jit(solution)/shard_map/psum | solution.py:263
  1369.5 285.5 %copy-start.13 = (bf16[2,1568,256]{2,1,0:T(8,128)(2,1)S(1)}, bf16[2,1568,256]{2,1,0:T(8,128)(2,1)}, u32[]{:S(2)}) copy-start(bf16[2,1568,256]{2,1,0:T(8,128)(2,1)} %copy-done.12) | copy-start | bytes 4816900
  1655.0 48.8 %copy-start.44 = (f32[784]{0:T(1024)S(1)}, f32[784]{0:T(1024)}, u32[]{:S(2)}) copy-start(f32[784]{0:T(1024)} %copy-done.43) | copy-start | bytes 9412
  (60 other events, 532.6 us)
Sparse Core Ops, SparseCore 0:
  10.2 101.8 all-gather.13
  114.3 47.4 all-gather.15
  164.0 123.4 all-gather.17
  289.4 123.5 all-gather.19
  513.0 87.3 reduce-scatter.6
  875.4 205.2 reduce-scatter.4
  1084.9 281.7 reduce-scatter.8
  1370.6 281.6 reduce-scatter.10
  1656.2 68.1 all-reduce.14
